TPU v7x, 32 devices: a whole 2x2x4 slice. The times are simulated.
32 devices in a mesh: section: 4 (over y, x), tile: 8 (over z, core).
Axes of the slice: x: 2, y: 2, z: 4, core: 2. Of those that a mesh axis runs over, the one named last changes fastest.
Arguments:
- features: bfloat16 [32, 16, 16, 256], P('tile'), may hold values from -6 to 6
- out_cotangent: bfloat16 [32, 16, 16, 256], P('tile'), may hold values from -6 to 6
- w_reduce: bfloat16 [4, 256, 64], P('section'), may hold values from -0.375 to 0.375
- w_taps: bfloat16 [4, 576, 64], P('section'), may hold values from -0.25 to 0.25
- w_expand: bfloat16 [4, 64, 256], P('section'), may hold values from -0.75 to 0.75
- norm_scale: float32 [4, 384], P('section'), may hold values from 0.25 to 1.75
- norm_shift: float32 [4, 384], P('section'), may hold values from -2 to 2
- owner: int32 [32], replicated, may hold values from 0 to 31, as said below
- neighbours: int32 [32, 4], replicated, may hold values from -1 to 31, as said below
Outputs:
- block_outputs: bfloat16 [4, 32, 16, 16, 256], P('section', 'tile')
- input_grads: bfloat16 [4, 32, 16, 16, 256], P('section', 'tile')
- grad_reduce: float32 [4, 256, 64], P('section')
- grad_taps: float32 [4, 576, 64], P('section')
- grad_expand: float32 [4, 64, 256], P('section')
Inputs may be any that keep to these rules, and one draw needn't show every extreme that they name: `owner`: A permutation of the rows; the rows 4 k to 4 k + 3 belong to index k of tile. The tiles form a band 8 tiles across; two neighbouring tiles are owned by indices of tile at most 3 apart, and west and east neighbours by indices at most 1 apart. Symmetric: if neighbours[t, 0] = u then neighbours[u, 1] = t, and likewise for west and east; -1 at the band's border.
All inputs are finite; a program needn't handle non-finite values.
Results may differ from a plain program's by a relative error of at most 0.039.
Values may be sent and summed in bfloat16 or wider, within the bound.
A program may use at most 64 MiB of HBM per device.

v0:
```python
from functools import partial

import jax
import jax.numpy as jnp
import numpy as np
from jax import lax
from jax.experimental import pallas as pl
from jax.experimental.pallas import tpu as pltpu
from jax.sharding import PartitionSpec as P

REACH = 3
SPAN = 2 * REACH + 1
MESH = pl.DeviceIdType.MESH
SIDE = 16
PIX = SIDE * SIDE
EXT = PIX + 2 * SIDE
FULL = EXT + 2 * SIDE
REGIONS = (416, 128)


def shift_matrices():
    left = np.zeros((EXT, FULL), np.float32)
    right = np.zeros((EXT, FULL), np.float32)
    for r in range(EXT):
        y, x = r // SIDE - 1, r % SIDE
        inside = 0 <= y < SIDE
        if x > 0:
            left[r, r - 1] = 1
        elif inside:
            left[r, EXT + y] = 1
        if x < SIDE - 1:
            right[r, r + 1] = 1
        elif inside:
            right[r, EXT + SIDE + y] = 1
    face = np.zeros((4 * SIDE, PIX), np.float32)
    for i in range(SIDE):
        face[i, i] = 1
        face[SIDE + i, PIX - SIDE + i] = 1
        face[2 * SIDE + i, SIDE * i] = 1
        face[3 * SIDE + i, SIDE * i + SIDE - 1] = 1
    return np.concatenate([left, right]), face


def sigmoid(v):
    return 0.5 * jnp.tanh(0.5 * v) + 0.5


def mm(left, right):
    return jnp.dot(left, right, preferred_element_type=jnp.float32)


def mm_t(left, right):
    return lax.dot_general(
        left, right, (((1,), (1,)), ((), ())), preferred_element_type=jnp.float32
    )


def t_mm(left, right):
    return lax.dot_general(
        left, right, (((0,), (0,)), ((), ())), preferred_element_type=jnp.float32
    )


def kernel(
    n, blocks, chunks, counts,
    owner_ref, near_ref, feat_ref, cot_ref, w1_ref, wt_ref, w3_ref, sc_ref, sh_ref,
    inner_in, rim_in, inner_t_in, rim_t_in, face_in, face_t_in,
    out_ref, din_ref, gr_ref, gt_ref, ge_ref,
    sel, inner_ref, rim_ref, inner_t_ref, rim_t_ref, face_ref, face_t_ref, acts, dins, W1, WT, W3, WC, NS, NT,
    D1, D2, D3, pre2_s, pre3_s, CAT, H2, DD3, F, SEND, RECV, HELD, G0, G1, RS0, RS1, PART0, PART1, SG0, SG1, FIN0, FIN1,
    load_sem, const_sem, wl_sem, ws_sem, wr_sem, xs_sem, xr_sem,
    os_sem, or_sem, ol_sem, *grad_sems,
):
    s = lax.axis_index("section")
    k = lax.axis_index("tile")
    lo = jnp.maximum(k - REACH, 0)
    hi = jnp.minimum(k + REACH + 1, n)
    bf = jnp.bfloat16

    feat_copy = pltpu.make_async_copy(feat_ref.at[s], acts.at[0], load_sem.at[0])
    cot_copy = pltpu.make_async_copy(cot_ref.at[s], dins.at[blocks], load_sem.at[1])
    const_copies = [
        pltpu.make_async_copy(src, dst, const_sem.at[i])
        for i, (src, dst) in enumerate([
            (face_in, face_ref), (inner_in, inner_ref), (rim_in, rim_ref),
            (inner_t_in, inner_t_ref), (rim_t_in, rim_t_ref), (face_t_in, face_t_ref),
        ])
    ]
    feat_copy.start()
    weights = [
        (w1_ref.at[0], W1), (sc_ref, NS), (sh_ref, NT), (wt_ref.at[0], WT), (w3_ref.at[0], W3)
    ]
    for i, (src, dst) in enumerate(weights):
        pltpu.make_async_copy(src, dst.at[s], wl_sem.at[i]).start()
    for copy in const_copies:
        copy.start()
    cot_copy.start()

    barrier = pltpu.get_barrier_semaphore()

    def greet(kk, total):
        near = jnp.logical_and(kk >= lo, kk < hi)
        for ss in range(blocks):
            go = jnp.logical_and(
                jnp.logical_or(near, s == ss), jnp.logical_not(jnp.logical_and(s == ss, kk == k))
            )

            @pl.when(go)
            def _():
                pl.semaphore_signal(barrier, inc=1, device_id=(ss, kk), device_id_type=MESH)

        return total

    lax.fori_loop(0, n, greet, 0)
    slot = k * blocks + s
    tiles = owner_ref.shape[0]
    tile = lax.fori_loop(
        0, tiles, lambda i, acc: jnp.where(owner_ref[i] == slot, i, acc), jnp.int32(0)
    )
    places, valids = [], []
    for j in range(4):
        near = near_ref[j, tile]
        valid = near >= 0
        where = owner_ref[jnp.where(valid, near, 0)]
        hop = lax.rem(where % blocks - s + blocks, blocks)
        place = (where // blocks - k + REACH) * blocks + hop
        place = jnp.where(valid, place, 0)
        places.append(jnp.clip(place, 0, SPAN * blocks - 1))
        valids.append(valid)
    for i in range(SPAN * blocks):
        pick = jnp.int32(0)
        for j in range(1, 4):
            pick = jnp.where(jnp.logical_and(valids[j], places[j] == i), j, pick)
        sel[i] = pick

    pl.semaphore_wait(barrier, (hi - lo) * (blocks - 1) + n - 1)

    def weight_copy(i, target, slot):
        src, dst = weights[i]
        return pltpu.make_async_remote_copy(
            src_ref=src, dst_ref=dst.at[slot],
            send_sem=ws_sem.at[i, target], recv_sem=wr_sem.at[i, slot],
            device_id=(target, k), device_id_type=MESH,
        )

    def send_weights():
        for i in range(len(weights)):
            for target in range(blocks):
                @pl.when(s != target)
                def _():
                    weight_copy(i, target, s).start()

    @pl.when(s == 0)
    def _():
        send_weights()

    def partners():
        for far in sorted(range(-REACH, REACH + 1), key=lambda o: -abs(o)):
            yield far, [hop for hop in range(blocks) if far or hop]

    def exchange_copy(par, far, hop):
        theirs = (far + REACH) * blocks + hop
        mine = (REACH - far) * blocks + (blocks - hop) % blocks
        return pltpu.make_async_remote_copy(
            src_ref=SEND.at[par, theirs], dst_ref=RECV.at[par, mine],
            send_sem=xs_sem.at[par, theirs], recv_sem=xr_sem.at[par, mine],
            device_id=(lax.rem(s + hop, blocks), k + far), device_id_type=MESH,
        )

    def each_partner(action):
        for far, hops in partners():
            def body():
                for hop in hops:
                    action(far, hop)

            if far:
                pl.when(jnp.logical_and(k + far >= 0, k + far < n))(body)
            else:
                body()

    def sent(par):
        each_partner(lambda far, hop: exchange_copy(par, far, hop).wait_send())

    def start_exchange(par, faces):
        F[...] = jnp.concatenate([faces, faces], axis=1).reshape(4, SIDE, 128)
        for i in range(SPAN * blocks):
            SEND[par, i] = F[sel[i]]
        each_partner(lambda far, hop: exchange_copy(par, far, hop).start())

    def end_exchange(par):
        each_partner(lambda far, hop: exchange_copy(par, -far, -hop % blocks).wait_recv())
        HELD[...] = RECV[par]
        got = []
        for j in range(4):
            face = HELD[places[j]][:, :64]
            got.append(jnp.where(valids[j], face.astype(jnp.float32), 0.0).astype(bf))
        return got

    def result_copy(which, b, ref, src):
        return pltpu.make_async_remote_copy(
            src_ref=src, dst_ref=ref.at[s],
            send_sem=os_sem.at[which, b], recv_sem=or_sem.at[which, s],
            device_id=(b, k), device_id_type=MESH,
        )

    def result_local(which, ref, src):
        return pltpu.make_async_copy(src, ref.at[s], ol_sem.at[which])

    def send_result(which, b, ref, src):
        @pl.when(b != s)
        def _():
            result_copy(which, b, ref, src).start()

        @pl.when(b == s)
        def _():
            result_local(which, ref, src).start()

    def derivative(v):
        sig = sigmoid(v)
        return sig * (1.0 + v * (1.0 - sig))

    def tail_derivatives(b):
        D2[b] = derivative(pre2_s[...]) * NS[b][:, 64:128]
        D3[b] = derivative(pre3_s[...])

    for i, (src, dst) in enumerate(weights):
        pltpu.make_async_copy(src, dst.at[s], wl_sem.at[i]).wait()
    feat_copy.wait()
    for copy in const_copies:
        copy.wait()

    def forward(b, carry):
        par = lax.rem(b, 2)

        @pl.when(b != s)
        def _():
            for i in range(len(weights)):
                weight_copy(i, b, b).wait_recv()

        a = acts[b]
        scale = NS[b]
        shift = NT[b]
        pre1 = mm_t(a, W1[b]) * scale[:, :64] + shift[:, :64]
        sig = sigmoid(pre1)
        h1 = (pre1 * sig).astype(bf)
        start_exchange(par, mm(face_ref[...], h1).astype(bf))

        @pl.when(b > 0)
        def _():
            sent(1 - par)
            send_result(0, b - 1, out_ref, acts.at[b])
            tail_derivatives(b - 1)

        @pl.when(jnp.logical_and(b == 0, s != 0))
        def _():
            send_weights()

        D1[b] = sig * (1.0 + pre1 * (1.0 - sig)) * scale[:, :64]
        taps = WT[b]
        WC[b] = jnp.concatenate([taps[:, :192], taps[:, 192:384], taps[:, 384:]], axis=0)
        moved = mm(inner_ref[...], h1)

        got = end_exchange(par)
        full = jnp.concatenate([got[0], h1, got[1]], axis=0)
        moved = (moved + mm(rim_ref[...], jnp.concatenate(got, axis=0))).astype(bf)
        cat = jnp.concatenate([moved[:EXT], full, moved[EXT:]], axis=1)
        CAT[b] = cat
        rows = mm_t(cat, WC[b])
        pre2 = (
            rows[:PIX, :64] + rows[SIDE : SIDE + PIX, 64:128] + rows[2 * SIDE :, 128:]
        )
        pre2 = pre2 * scale[:, 64:128] + shift[:, 64:128]
        pre2_s[...] = pre2
        h2 = (pre2 * sigmoid(pre2)).astype(bf)
        H2[b] = h2
        pre3 = a.astype(jnp.float32) + mm(h2, W3[b]) * scale[:, 128:] + shift[:, 128:]
        pre3_s[...] = pre3
        acts[b + 1] = (pre3 * sigmoid(pre3)).astype(bf)
        return carry

    lax.fori_loop(0, blocks, forward, 0)
    tail_derivatives(blocks - 1)
    cot_copy.wait()

    grads = [
        (G0, RS0, PART0, SG0, FIN0, chunks[0], counts[0]) + grad_sems[:6],
        (G1, RS1, PART1, SG1, FIN1, chunks[1], counts[1]) + grad_sems[6:],
    ]

    def others(count, action):
        def body(kk, carry):
            @pl.when(kk != k)
            def _():
                action(kk)

            return carry

        lax.fori_loop(0, count, body, 0)

    def piece(r, b, kk):
        chunk = grads[r][5]
        return grads[r][0].at[b, pl.ds(pl.multiple_of(kk * chunk, 16), chunk)]

    def to_owner(r, b, kk):
        return pltpu.make_async_remote_copy(
            src_ref=piece(r, b, kk), dst_ref=grads[r][1].at[b, k],
            send_sem=grads[r][7].at[b, kk], recv_sem=grads[r][8].at[b, k],
            device_id=(s, kk), device_id_type=MESH,
        )

    def from_peer(r, b, kk):
        slot = grads[r][1].at[b, kk]
        return pltpu.make_async_remote_copy(
            src_ref=slot, dst_ref=slot,
            send_sem=grads[r][7].at[b, 0], recv_sem=grads[r][8].at[b, kk],
            device_id=(s, kk), device_id_type=MESH,
        )

    def to_section(r, b, slot):
        return pltpu.make_async_remote_copy(
            src_ref=grads[r][2].at[b], dst_ref=grads[r][3].at[slot],
            send_sem=grads[r][9].at[b], recv_sem=grads[r][10].at[slot],
            device_id=(b, k), device_id_type=MESH,
        )

    def final_copy(r, kk, slot):
        return pltpu.make_async_remote_copy(
            src_ref=grads[r][4].at[slot], dst_ref=grads[r][4].at[slot],
            send_sem=grads[r][11].at[kk], recv_sem=grads[r][12].at[slot],
            device_id=(s, kk), device_id_type=MESH,
        )

    def scatter(r, b):
        others(counts[r], lambda kk: to_owner(r, b, kk).start())

    def owner_sum(r, b):
        G, RS, PART, SG = grads[r][:4]
        chunk = chunks[r]

        @pl.when(k < counts[r])
        def _():
            RS[b, k] = G[b, pl.ds(pl.multiple_of(k * chunk, 16), chunk)]
            others(n, lambda kk: from_peer(r, b, kk).wait_recv())
            total = lax.fori_loop(
                0, n, lambda i, acc: acc + RS[b, i].astype(jnp.float32),
                jnp.zeros((chunk, 128), jnp.float32),
            ).astype(bf)

            @pl.when(b == s)
            def _():
                SG[s] = total

            @pl.when(b != s)
            def _():
                PART[b] = total
                to_section(r, b, s).start()

    def backward(step, carry):
        b = blocks - 1 - step
        par = lax.rem(step + blocks, 2)
        scale = NS[b]
        d3 = dins[b + 1].astype(jnp.float32) * D3[b]
        DD3[...] = d3
        e3 = (d3 * scale[:, 128:]).astype(bf)
        d2 = (mm_t(e3, W3[b]) * D2[b]).astype(bf)
        zero = jnp.zeros((SIDE, 64), bf)
        d2cat = jnp.concatenate(
            [
                jnp.concatenate([d2, zero, zero], axis=0),
                jnp.concatenate([zero, d2, zero], axis=0),
                jnp.concatenate([zero, zero, d2], axis=0),
            ],
            axis=1,
        )
        dcat = mm(d2cat, WC[b])
        sides = jnp.concatenate([dcat[:, :64], dcat[:, 128:]], axis=0).astype(bf)
        drim = mm(rim_t_ref[...], sides)
        mid = dcat[:, 64:128]
        faces = jnp.concatenate(
            [drim[:SIDE] + mid[:SIDE], drim[SIDE : 2 * SIDE] + mid[SIDE + PIX :], drim[2 * SIDE :]],
            axis=0,
        )
        start_exchange(par, faces.astype(bf))
        dmid = (mm(inner_t_ref[...], sides) + mid[SIDE : SIDE + PIX]).astype(bf)
        taps = t_mm(d2cat, CAT[b]).astype(bf)
        G0[b, :192] = taps[:, :128]
        G0[b, 192:288] = jnp.concatenate([taps[:96, 128:], taps[96:, 128:]], axis=1)
        expand = t_mm(H2[b], e3).astype(bf)
        G0[b, 288:352] = expand[:, :128]
        G0[b, 352:416] = expand[:, 128:]
        spare = counts[0] * chunks[0] - REGIONS[0]
        if spare:
            G0[b, REGIONS[0] :] = jnp.zeros((spare, 128), bf)
        scatter(0, b)
        sent(1 - par)

        @pl.when(step == 0)
        def _():
            send_result(0, blocks - 1, out_ref, acts.at[blocks])

        @pl.when(step > 0)
        def _():
            send_result(1, b + 1, din_ref, dins.at[b + 1])
            owner_sum(0, b + 1)
            owner_sum(1, b + 1)

        got = end_exchange(par)
        dh1 = dmid.astype(jnp.float32) + mm(
            face_t_ref[...], jnp.concatenate(got, axis=0)
        )
        d1 = (dh1 * D1[b]).astype(bf)
        red = t_mm(d1, acts[b]).astype(bf)
        G1[b, :64] = red[:, :128]
        G1[b, 64:] = red[:, 128:]
        scatter(1, b)
        dins[b] = (DD3[...] + mm(d1, W1[b])).astype(bf)
        return carry

    lax.fori_loop(0, blocks, backward, 0)
    send_result(1, 0, din_ref, dins.at[0])
    sent((2 * blocks - 1) % 2)

    for r in (0, 1):
        owner_sum(r, 0)
    for r in (0, 1):
        SG, FIN = grads[r][3:5]

        @pl.when(k < counts[r])
        def _():
            for ss in range(blocks):
                @pl.when(s != ss)
                def _():
                    to_section(r, ss, ss).wait_recv()

            FIN[k] = sum(SG[ss].astype(jnp.float32) for ss in range(blocks)).astype(bf)
            others(n, lambda kk: final_copy(r, kk, k).start())

    for r in (0, 1):
        others(counts[r], lambda kk: final_copy(r, kk, kk).wait_recv())
    done = FIN0[...].reshape(counts[0] * chunks[0], 128).astype(jnp.float32)
    red = FIN1[...].reshape(REGIONS[1], 128).astype(jnp.float32)
    right = jnp.concatenate([done[192:288, :64], done[192:288, 64:]], axis=0)
    for dy in range(3):
        span = slice(64 * dy, 64 * dy + 64)
        gt_ref[0, :, 192 * dy : 192 * dy + 192] = jnp.concatenate(
            [done[span], right[span]], axis=1
        )
    ge_ref[0, :, :128] = done[288:352]
    ge_ref[0, :, 128:] = done[352:416]
    gr_ref[0, :, :128] = red[:64]
    gr_ref[0, :, 128:] = red[64:]

    for r in (0, 1):
        for b in range(blocks):
            others(counts[r], lambda kk: to_owner(r, b, kk).wait_send())

        @pl.when(k < counts[r])
        def _():
            others(n, lambda kk: final_copy(r, kk, k).wait_send())
            for ss in range(blocks):
                @pl.when(s != ss)
                def _():
                    to_section(r, ss, ss).wait_send()

    for ss in range(blocks):
        @pl.when(s != ss)
        def _():
            for i in range(len(weights)):
                weight_copy(i, ss, ss).wait_send()
            for which, ref, held in ((0, out_ref, acts.at[ss + 1]), (1, din_ref, dins.at[ss])):
                pltpu.make_async_remote_copy(
                    src_ref=held, dst_ref=ref.at[ss],
                    send_sem=os_sem.at[which, ss], recv_sem=or_sem.at[which, ss],
                    device_id=(ss, k), device_id_type=MESH,
                ).wait()

    result_local(0, out_ref, acts.at[s + 1]).wait()
    result_local(1, din_ref, dins.at[s]).wait()


def copy_out(*refs):
    sems = refs[10]
    copies = [pltpu.make_async_copy(refs[i], refs[5 + i], sems.at[i]) for i in range(5)]
    for copy in copies:
        copy.start()
    for copy in copies:
        copy.wait()


def on_device(
    features, out_cotangent, w_reduce, w_taps, w_expand, norm_scale, norm_shift, owner, neighbours
):
    blocks = lax.axis_size("section")
    n = lax.axis_size("tile")
    slots, side, _, chans = features.shape
    bf, f32 = jnp.bfloat16, jnp.float32
    chunks = [16 * max(1, -(-rows // (16 * n))) for rows in REGIONS]
    counts = [-(-rows // chunk) for rows, chunk in zip(REGIONS, chunks)]
    shift, face = shift_matrices()
    inner = shift[:, SIDE : SIDE + PIX]
    rim = np.concatenate([shift[:, :SIDE], shift[:, SIDE + PIX :]], axis=1)
    consts = [jnp.asarray(m, bf) for m in (inner, rim, inner.T, rim.T, face, face.T)]
    vmem = pl.BlockSpec(memory_space=pltpu.VMEM)
    smem = pl.BlockSpec(memory_space=pltpu.SMEM)
    anyw = pl.BlockSpec(memory_space=pl.ANY)
    hbm = pl.BlockSpec(memory_space=pltpu.HBM)
    dma = pltpu.SemaphoreType.DMA
    spots = SPAN * blocks
    results = pl.pallas_call(
        partial(kernel, n, blocks, chunks, counts),
        out_shape=(
            jax.ShapeDtypeStruct((slots, PIX, chans), bf),
            jax.ShapeDtypeStruct((slots, PIX, chans), bf),
            jax.ShapeDtypeStruct((1, 64, 256), f32),
            jax.ShapeDtypeStruct((1, 64, 576), f32),
            jax.ShapeDtypeStruct((1, 64, 256), f32),
        ),
        in_specs=[smem] * 2 + [hbm] * 13,
        out_specs=[anyw] * 2 + [vmem] * 3,
        scratch_shapes=[
            pltpu.SMEM((spots,), jnp.int32),
            *[pltpu.VMEM(m.shape, bf) for m in consts],
            pltpu.VMEM((blocks + 1, PIX, chans), bf),
            pltpu.VMEM((blocks + 1, PIX, chans), bf),
            pltpu.VMEM((blocks, 64, 256), bf),
            pltpu.VMEM((blocks, 64, 576), bf),
            pltpu.VMEM((blocks, 64, 256), bf),
            pltpu.VMEM((blocks, 192, 192), bf),
            pltpu.VMEM((blocks, 1, 384), f32),
            pltpu.VMEM((blocks, 1, 384), f32),
            pltpu.VMEM((blocks, PIX, 64), f32),
            pltpu.VMEM((blocks, PIX, 64), f32),
            pltpu.VMEM((blocks, PIX, chans), f32),
            pltpu.VMEM((PIX, 64), f32),
            pltpu.VMEM((PIX, chans), f32),
            pltpu.VMEM((blocks, EXT, 192), bf),
            pltpu.VMEM((blocks, PIX, 64), bf),
            pltpu.VMEM((PIX, chans), f32),
            pltpu.VMEM((4, SIDE, 128), bf),
            pltpu.VMEM((2, spots, SIDE, 128), bf),
            pltpu.VMEM((2, spots, SIDE, 128), bf),
            pltpu.VMEM((spots, SIDE, 128), bf),
            *[pltpu.VMEM((blocks, c * m, 128), bf) for c, m in zip(chunks, counts)],
            *[pltpu.VMEM((blocks, n, c, 128), bf) for c in chunks],
            *[pltpu.VMEM((blocks, c, 128), bf) for c in chunks],
            *[pltpu.VMEM((blocks, c, 128), bf) for c in chunks],
            *[pltpu.VMEM((m, c, 128), bf) for c, m in zip(chunks, counts)],
            dma((2,)), dma((6,)), dma((5,)), dma((5, blocks)), dma((5, blocks)),
            dma((2, spots)), dma((2, spots)),
            dma((2, blocks)), dma((2, blocks)), dma((2,)),
            *[
                dma(shape)
                for m in counts
                for shape in ((blocks, m), (blocks, n), (blocks,), (blocks,), (n,), (m,))
            ],
        ],
        compiler_params=pltpu.CompilerParams(
            collective_id=0, has_side_effects=True, vmem_limit_bytes=60 * 1024 * 1024
        ),
        name="residual_blocks",
    )(
        owner, neighbours.T,
        features.reshape(slots, PIX, chans), out_cotangent.reshape(slots, PIX, chans),
        jnp.swapaxes(w_reduce, 1, 2), jnp.swapaxes(w_taps, 1, 2), w_expand, norm_scale, norm_shift,
        *consts,
    )
    results = pl.pallas_call(
        copy_out,
        out_shape=tuple(jax.ShapeDtypeStruct(r.shape, r.dtype) for r in results),
        in_specs=[anyw] * 5,
        out_specs=[anyw] * 5,
        scratch_shapes=[dma((5,))],
        name="copy_out",
    )(*results)
    shape = (1, slots, side, side, chans)
    return (
        results[0].reshape(shape), results[1].reshape(shape),
        jnp.swapaxes(results[2], 1, 2), jnp.swapaxes(results[3], 1, 2), results[4],
    )


def solution(mesh):
    return jax.shard_map(
        on_device,
        mesh=mesh,
        in_specs=(
            P("tile", None, None, None),
            P("tile", None, None, None),
            P("section", None, None),
            P("section", None, None),
            P("section", None, None),
            P("section", None),
            P("section", None),
            P(),
            P(),
        ),
        out_specs=(
            P("section", "tile", None, None, None),
            P("section", "tile", None, None, None),
            P("section", None, None),
            P("section", None, None),
            P("section", None, None),
        ),
        check_vma=False,
    )
```

profile of v0, /device:TPU:0, one launch (start us, length us, event | category | flops | bytes accessed | tf_op | source)
XLA Modules:
  0.0 129.2 jit_solution(7291373426384761471)
XLA Ops:
  0.6 86.7 %residual_blocks.1 = (bf16[4,256,256]{2,1,0:T(8,128)(2,1)}, bf16[4,256,256]{2,1,0:T(8,128)(2,1)}, f32[1,64,256]{2,1,0:T(8,128)}, f32[1,64,576]{2,1,0:T(8,128)}, f32[1,64,256]{2,1,0:T(8,128)}) custom-call(s32[32]{0:T(128)} %owner_ref.1, s32[4,32]{1,0:T(4,128)} %bitcast.13, bf16[4,256,256]{2,1,0:T(8,128)(2,1)} %bitcast.9, bf16[4,256,256]{2,1,0:T(8,128)(2,1)} %bitcast.10, ...), custom_call_target="tpu_custom_call" | custom-call | tf_op jit(solution)/shard_map/residual_blocks/pallas_call | solution.py:509
  87.4 41.8 %copy_out.1 = (bf16[4,256,256]{2,1,0:T(8,128)(2,1)}, bf16[4,256,256]{2,1,0:T(8,128)(2,1)}, f32[1,64,256]{2,1,0:T(8,128)}, f32[1,64,576]{2,1,0:T(8,128)}, f32[1,64,256]{2,1,0:T(8,128)}) custom-call(bf16[4,256,256]{2,1,0:T(8,128)(2,1)} %get-tuple-element.15.refs_0_, bf16[4,256,256]{2,1,0:T(8,128)(2,1)} %get-tuple-element.16.refs_1_, ...), custom_call_target="tpu_custom_call" | custom-call | tf_op jit(solution)/shard_map/copy_out/pallas_call | solution.py:567
where the time goes:
time: 129 us
  Pallas kernels  129 us (100%)
    pallas_call x1, Pallas kernels, on_device(): pl.pallas_call(partial(kernel, n, blocks, chunks, counts), out_shape=(jax...  86.7 us
    pallas_call x1, Pallas kernels, on_device(): pl.pallas_call(copy_out, out_shape=tuple((jax.ShapeDtypeStruct(r.shape, r...  41.8 us

commit v1 on v0

--- a/solution.py
+++ b/solution.py
@@ -196,24 +196,27 @@
             got.append(jnp.where(valids[j], face.astype(jnp.float32), 0.0).astype(bf))
         return got
 
-    def result_copy(which, b, ref, src):
+    def result_copy(which, b, ref, src, half, slot):
+        rows = pl.ds(half * (PIX // 2), PIX // 2)
         return pltpu.make_async_remote_copy(
-            src_ref=src, dst_ref=ref.at[s],
-            send_sem=os_sem.at[which, b], recv_sem=or_sem.at[which, s],
+            src_ref=src.at[rows], dst_ref=ref.at[slot, rows],
+            send_sem=os_sem.at[which, b, half], recv_sem=or_sem.at[which, slot, half],
             device_id=(b, k), device_id_type=MESH,
         )
 
     def result_local(which, ref, src):
         return pltpu.make_async_copy(src, ref.at[s], ol_sem.at[which])
 
-    def send_result(which, b, ref, src):
+    def send_result(which, b, ref, src, halves=(0, 1)):
         @pl.when(b != s)
         def _():
-            result_copy(which, b, ref, src).start()
-
-        @pl.when(b == s)
-        def _():
-            result_local(which, ref, src).start()
+            for half in halves:
+                result_copy(which, b, ref, src, half, s).start()
+
+        if 0 in halves:
+            @pl.when(b == s)
+            def _():
+                result_local(which, ref, src).start()
 
     def derivative(v):
         sig = sigmoid(v)
@@ -417,11 +420,12 @@
         return carry
 
     lax.fori_loop(0, blocks, backward, 0)
-    send_result(1, 0, din_ref, dins.at[0])
+    send_result(1, 0, din_ref, dins.at[0], (0,))
     sent((2 * blocks - 1) % 2)
 
     for r in (0, 1):
         owner_sum(r, 0)
+    send_result(1, 0, din_ref, dins.at[0], (1,))
     for r in (0, 1):
         SG, FIN = grads[r][3:5]
 
@@ -468,22 +472,28 @@
             for i in range(len(weights)):
                 weight_copy(i, ss, ss).wait_send()
             for which, ref, held in ((0, out_ref, acts.at[ss + 1]), (1, din_ref, dins.at[ss])):
-                pltpu.make_async_remote_copy(
-                    src_ref=held, dst_ref=ref.at[ss],
-                    send_sem=os_sem.at[which, ss], recv_sem=or_sem.at[which, ss],
-                    device_id=(ss, k), device_id_type=MESH,
-                ).wait()
+                for half in (0, 1):
+                    result_copy(which, ss, ref, held, half, ss).wait()
 
     result_local(0, out_ref, acts.at[s + 1]).wait()
     result_local(1, din_ref, dins.at[s]).wait()
 
 
 def copy_out(*refs):
-    sems = refs[10]
-    copies = [pltpu.make_async_copy(refs[i], refs[5 + i], sems.at[i]) for i in range(5)]
-    for copy in copies:
+    held, load, store = refs[10:15], refs[15], refs[16]
+    pieces = [
+        (refs[i].at[part], held[i].at[part], refs[5 + i].at[part])
+        for i in range(5)
+        for part in range(refs[i].shape[0])
+    ]
+    loads = [pltpu.make_async_copy(p[0], p[1], load.at[i]) for i, p in enumerate(pieces)]
+    stores = [pltpu.make_async_copy(p[1], p[2], store.at[i]) for i, p in enumerate(pieces)]
+    for copy in loads:
         copy.start()
-    for copy in copies:
+    for before, after in zip(loads, stores):
+        before.wait()
+        after.start()
+    for copy in stores:
         copy.wait()
 
 
@@ -547,7 +557,7 @@
             *[pltpu.VMEM((m, c, 128), bf) for c, m in zip(chunks, counts)],
             dma((2,)), dma((6,)), dma((5,)), dma((5, blocks)), dma((5, blocks)),
             dma((2, spots)), dma((2, spots)),
-            dma((2, blocks)), dma((2, blocks)), dma((2,)),
+            dma((2, blocks, 2)), dma((2, blocks, 2)), dma((2,)),
             *[
                 dma(shape)
                 for m in counts
@@ -569,7 +579,10 @@
         out_shape=tuple(jax.ShapeDtypeStruct(r.shape, r.dtype) for r in results),
         in_specs=[anyw] * 5,
         out_specs=[anyw] * 5,
-        scratch_shapes=[dma((5,))],
+        scratch_shapes=[
+            *[pltpu.VMEM(r.shape, r.dtype) for r in results],
+            dma((2 * slots + 3,)), dma((2 * slots + 3,)),
+        ],
         name="copy_out",
     )(*results)
     shape = (1, slots, side, side, chans)

time: 129 us -> 88.6 us (0.69)
  Pallas kernels: 129 us -> 87.7 us
    pallas_call x1, Pallas kernels: 41.8 us -> 2.23 us  [on_device(): pl.pallas_call(copy_out, out_shape=tuple((jax.ShapeDtypeStruct(r.shape, r...]
where the time goes in v1:
time: 88.6 us; the launch traced here: 88.3 us
  Pallas kernels  87.7 us (99%)
    pallas_call x1, Pallas kernels, on_device(): pl.pallas_call(partial(kernel, n, blocks, chunks, counts), out_shape=(jax...  85.4 us
    pallas_call x1, Pallas kernels, on_device(): pl.pallas_call(copy_out, out_shape=tuple((jax.ShapeDtypeStruct(r.shape, r...  2.23 us

profile of v1, /device:TPU:0, one launch (start us, length us, event | category | flops | bytes accessed | tf_op | source)
XLA Modules:
  0.0 88.3 jit_solution(10258761526690956250)
XLA Ops:
  0.6 85.4 %residual_blocks.1 = (bf16[4,256,256]{2,1,0:T(8,128)(2,1)}, bf16[4,256,256]{2,1,0:T(8,128)(2,1)}, f32[1,64,256]{2,1,0:T(8,128)}, f32[1,64,576]{2,1,0:T(8,128)}, f32[1,64,256]{2,1,0:T(8,128)}) custom-call(s32[32]{0:T(128)} %owner_ref.1, s32[4,32]{1,0:T(4,128)} %bitcast.13, bf16[4,256,256]{2,1,0:T(8,128)(2,1)} %bitcast.9, bf16[4,256,256]{2,1,0:T(8,128)(2,1)} %bitcast.10, ...), custom_call_target="tpu_custom_call" | custom-call | tf_op jit(solution)/shard_map/residual_blocks/pallas_call | solution.py:519
  86.1 2.2 %copy_out.1 = (bf16[4,256,256]{2,1,0:T(8,128)(2,1)}, bf16[4,256,256]{2,1,0:T(8,128)(2,1)}, f32[1,64,256]{2,1,0:T(8,128)}, f32[1,64,576]{2,1,0:T(8,128)}, f32[1,64,256]{2,1,0:T(8,128)}) custom-call(bf16[4,256,256]{2,1,0:T(8,128)(2,1)} %get-tuple-element.15.refs_0_, bf16[4,256,256]{2,1,0:T(8,128)(2,1)} %get-tuple-element.16.refs_1_, ...), custom_call_target="tpu_custom_call" | custom-call | tf_op jit(solution)/shard_map/copy_out/pallas_call | solution.py:577

commit v2 on v1

--- a/solution.py
+++ b/solution.py
@@ -67,7 +67,7 @@
     inner_in, rim_in, inner_t_in, rim_t_in, face_in, face_t_in,
     out_ref, din_ref, gr_ref, gt_ref, ge_ref,
     sel, inner_ref, rim_ref, inner_t_ref, rim_t_ref, face_ref, face_t_ref, acts, dins, W1, WT, W3, WC, NS, NT,
-    D1, D2, D3, pre2_s, pre3_s, CAT, H2, DD3, F, SEND, RECV, HELD, G0, G1, RS0, RS1, PART0, PART1, SG0, SG1, FIN0, FIN1,
+    D1, D2, D3, pre2_s, pre3_s, CAT, H2, DD1, DD3, F, SEND, RECV, HELD, G0, G1, RS0, RS1, PART0, PART1, SG0, SG1, FIN0, FIN1,
     load_sem, const_sem, wl_sem, ws_sem, wr_sem, xs_sem, xr_sem,
     os_sem, or_sem, ol_sem, *grad_sems,
 ):
@@ -358,6 +358,12 @@
                 PART[b] = total
                 to_section(r, b, s).start()
 
+    def late_grads(b):
+        red = t_mm(DD1[...], acts[b]).astype(bf)
+        G1[b, :64] = red[:, :128]
+        G1[b, 64:] = red[:, 128:]
+        scatter(1, b)
+
     def backward(step, carry):
         b = blocks - 1 - step
         par = lax.rem(step + blocks, 2)
@@ -404,23 +410,26 @@
         @pl.when(step > 0)
         def _():
             send_result(1, b + 1, din_ref, dins.at[b + 1])
+            late_grads(b + 1)
             owner_sum(0, b + 1)
-            owner_sum(1, b + 1)
+
+        @pl.when(step > 1)
+        def _():
+            owner_sum(1, b + 2)
 
         got = end_exchange(par)
         dh1 = dmid.astype(jnp.float32) + mm(
             face_t_ref[...], jnp.concatenate(got, axis=0)
         )
         d1 = (dh1 * D1[b]).astype(bf)
-        red = t_mm(d1, acts[b]).astype(bf)
-        G1[b, :64] = red[:, :128]
-        G1[b, 64:] = red[:, 128:]
-        scatter(1, b)
+        DD1[...] = d1
         dins[b] = (DD3[...] + mm(d1, W1[b])).astype(bf)
         return carry
 
     lax.fori_loop(0, blocks, backward, 0)
+    late_grads(0)
     send_result(1, 0, din_ref, dins.at[0], (0,))
+    owner_sum(1, 1)
     sent((2 * blocks - 1) % 2)
 
     for r in (0, 1):
@@ -545,6 +554,7 @@
             pltpu.VMEM((PIX, chans), f32),
             pltpu.VMEM((blocks, EXT, 192), bf),
             pltpu.VMEM((blocks, PIX, 64), bf),
+            pltpu.VMEM((PIX, 64), bf),
             pltpu.VMEM((PIX, chans), f32),
             pltpu.VMEM((4, SIDE, 128), bf),
             pltpu.VMEM((2, spots, SIDE, 128), bf),

time: 88.6 us -> 87.2 us (0.984)
  Pallas kernels: 87.7 us -> 86.4 us
    pallas_call x1, Pallas kernels: 85.4 us -> 84.2 us  [on_device(): pl.pallas_call(partial(kernel, n, blocks, chunks, counts), out_shape=(jax...]
where the time goes in v2:
time: 87.2 us; the launch traced here: 87.1 us
  Pallas kernels  86.4 us (99%)
    pallas_call x1, Pallas kernels, on_device(): pl.pallas_call(partial(kernel, n, blocks, chunks, counts), out_shape=(jax...  84.2 us
    pallas_call x1, Pallas kernels, on_device(): pl.pallas_call(copy_out, out_shape=tuple((jax.ShapeDtypeStruct(r.shape, r...  2.23 us

profile of v2, /device:TPU:0, one launch (start us, length us, event | category | flops | bytes accessed | tf_op | source)
XLA Modules:
  0.0 87.1 jit_solution(3205159204369193589)
XLA Ops:
  0.6 84.2 %residual_blocks.1 = (bf16[4,256,256]{2,1,0:T(8,128)(2,1)}, bf16[4,256,256]{2,1,0:T(8,128)(2,1)}, f32[1,64,256]{2,1,0:T(8,128)}, f32[1,64,576]{2,1,0:T(8,128)}, f32[1,64,256]{2,1,0:T(8,128)}) custom-call(s32[32]{0:T(128)} %owner_ref.1, s32[4,32]{1,0:T(4,128)} %bitcast.13, bf16[4,256,256]{2,1,0:T(8,128)(2,1)} %bitcast.9, bf16[4,256,256]{2,1,0:T(8,128)(2,1)} %bitcast.10, ...), custom_call_target="tpu_custom_call" | custom-call | tf_op jit(solution)/shard_map/residual_blocks/pallas_call | solution.py:528
  84.8 2.2 %copy_out.1 = (bf16[4,256,256]{2,1,0:T(8,128)(2,1)}, bf16[4,256,256]{2,1,0:T(8,128)(2,1)}, f32[1,64,256]{2,1,0:T(8,128)}, f32[1,64,576]{2,1,0:T(8,128)}, f32[1,64,256]{2,1,0:T(8,128)}) custom-call(bf16[4,256,256]{2,1,0:T(8,128)(2,1)} %get-tuple-element.15.refs_0_, bf16[4,256,256]{2,1,0:T(8,128)(2,1)} %get-tuple-element.16.refs_1_, ...), custom_call_target="tpu_custom_call" | custom-call | tf_op jit(solution)/shard_map/copy_out/pallas_call | solution.py:587

commit v3 on v2

--- a/solution.py
+++ b/solution.py
@@ -229,8 +229,7 @@
     for i, (src, dst) in enumerate(weights):
         pltpu.make_async_copy(src, dst.at[s], wl_sem.at[i]).wait()
     feat_copy.wait()
-    for copy in const_copies:
-        copy.wait()
+    const_copies[0].wait()
 
     def forward(b, carry):
         par = lax.rem(b, 2)
@@ -253,6 +252,11 @@
             sent(1 - par)
             send_result(0, b - 1, out_ref, acts.at[b])
             tail_derivatives(b - 1)
+
+        @pl.when(b == 0)
+        def _():
+            for copy in const_copies[1:]:
+                copy.wait()
 
         @pl.when(jnp.logical_and(b == 0, s != 0))
         def _():

time: 87.2 us -> 87.1 us (level)
  no operation moved by 1% of the time
where the time goes in v3:
time: 87.1 us; the launch traced here: 86.9 us
  Pallas kernels  86.3 us (99%)
    pallas_call x1, Pallas kernels, on_device(): pl.pallas_call(partial(kernel, n, blocks, chunks, counts), out_shape=(jax...  84.1 us
    pallas_call x1, Pallas kernels, on_device(): pl.pallas_call(copy_out, out_shape=tuple((jax.ShapeDtypeStruct(r.shape, r...  2.23 us

profile of v3, /device:TPU:0, one launch (start us, length us, event | category | flops | bytes accessed | tf_op | source)
XLA Modules:
  0.0 86.9 jit_solution(16726513442093591202)
XLA Ops:
  0.6 84.1 %residual_blocks.1 = (bf16[4,256,256]{2,1,0:T(8,128)(2,1)}, bf16[4,256,256]{2,1,0:T(8,128)(2,1)}, f32[1,64,256]{2,1,0:T(8,128)}, f32[1,64,576]{2,1,0:T(8,128)}, f32[1,64,256]{2,1,0:T(8,128)}) custom-call(s32[32]{0:T(128)} %owner_ref.1, s32[4,32]{1,0:T(4,128)} %bitcast.13, bf16[4,256,256]{2,1,0:T(8,128)(2,1)} %bitcast.9, bf16[4,256,256]{2,1,0:T(8,128)(2,1)} %bitcast.10, ...), custom_call_target="tpu_custom_call" | custom-call | tf_op jit(solution)/shard_map/residual_blocks/pallas_call | solution.py:532
  84.7 2.2 %copy_out.1 = (bf16[4,256,256]{2,1,0:T(8,128)(2,1)}, bf16[4,256,256]{2,1,0:T(8,128)(2,1)}, f32[1,64,256]{2,1,0:T(8,128)}, f32[1,64,576]{2,1,0:T(8,128)}, f32[1,64,256]{2,1,0:T(8,128)}) custom-call(bf16[4,256,256]{2,1,0:T(8,128)(2,1)} %get-tuple-element.15.refs_0_, bf16[4,256,256]{2,1,0:T(8,128)(2,1)} %get-tuple-element.16.refs_1_, ...), custom_call_target="tpu_custom_call" | custom-call | tf_op jit(solution)/shard_map/copy_out/pallas_call | solution.py:591
